TPU v7x, 32 devices: a whole 2x2x4 slice. The times are simulated.
32 devices in a mesh: cable: 2 (over y), blk: 4 (over z), sub: 4 (over x, core).
Axes of the slice: x: 2, y: 2, z: 4, core: 2. Of those that a mesh axis runs over, the one named last changes fastest.
Arguments:
- raw: bfloat16 [8, 8, 4096], P('cable', 'sub', 'blk'), parts along dimension 0, may hold values from -2500 to 2500
- valid: int32 [8, 8], P(('cable', 'blk'), 'sub'), parts along dimension 0, may hold values 0 or 1
- select: int32 [8, 4, 4], P(('cable', 'blk')), parts along dimension 0, may hold values 0 or 1
Outputs:
- corr: float32 [64, 4, 8, 512], P(('cable', 'blk'), None, 'sub'), parts along dimension 0
There are 2 independent parts, one for each index of `cable`. A program takes and returns all parts, laid end to end along the dimension named above; each array names one. Nothing has to cross between parts.
All inputs are finite; a program needn't handle non-finite values. No bound on the sum of `valid` or of `select` on one device may be relied on, other than what follows from the above.
Results may differ from a plain program's by a relative error of at most 0.0023.
Values may be sent and summed in bfloat16 or wider, within the bound.
A program may use at most 128 MiB of HBM per device.

v0:
```python
import math

import jax
import jax.numpy as jnp
from jax import lax
from jax.sharding import PartitionSpec as P

SEG_LEN = 1024
BAND = 64
LAGS = 512


eps = 1e-06


def dft_tables(length, bins):
    times = jnp.arange(length, dtype=jnp.int32)[:, None]
    freqs = jnp.arange(bins, dtype=jnp.int32)[None, :]
    angle = (times * freqs % length).astype(jnp.float32) * (2.0 * math.pi / length)
    return (jnp.cos(angle), -jnp.sin(angle))


def whiten(records, valid, seg_len, band):
    chans = records.shape[0] * records.shape[1]
    frames = records.astype(jnp.float32).reshape(chans, -1, seg_len)
    segs = frames.shape[1]
    bins = seg_len // 2
    cos_tab, sin_tab = dft_tables(seg_len, bins)
    real = jnp.einsum("cst,tf->csf", frames, cos_tab, precision=lax.Precision.HIGHEST)
    imag = jnp.einsum("cst,tf->csf", frames, sin_tab, precision=lax.Precision.HIGHEST)
    bands = bins // band
    power = (real * real + imag * imag).reshape(chans, segs, bands, band)
    level = jnp.mean(power, axis=(1, 3))
    factor = valid.reshape(chans, 1).astype(jnp.float32) / jnp.sqrt(level + eps)
    factor = factor[:, None, :, None]
    real = (real.reshape(chans, segs, bands, band) * factor).reshape(chans, segs, bins)
    imag = (imag.reshape(chans, segs, bands, band) * factor).reshape(chans, segs, bins)
    return jnp.stack([real, imag], axis=2).astype(jnp.bfloat16)


def lag_table(bins, lags, seg_len, scale):
    freqs = jnp.arange(bins, dtype=jnp.int32)[:, None]
    shifts = jnp.arange(lags, dtype=jnp.int32)[None, :] - lags // 2
    angle = (freqs * shifts % seg_len).astype(jnp.float32) * (2.0 * math.pi / seg_len)
    weight = jnp.where(freqs == 0, 1.0, 2.0).astype(jnp.float32) * scale
    return jnp.stack([weight * jnp.cos(angle), -weight * jnp.sin(angle)])


def pair_terms(own, weight_rows, piece):
    masked = piece * weight_rows.astype(jnp.bfloat16)[:, None, :, None, None]
    prod = jnp.einsum("isaf,njsbf->injabf", own, masked, preferred_element_type=jnp.float32)
    real = prod[:, :, :, 0, 0] + prod[:, :, :, 1, 1]
    imag = prod[:, :, :, 1, 0] - prod[:, :, :, 0, 1]
    return jnp.stack([real, imag], axis=3)


def per_device(raw, valid, select):
    regrouped = lax.all_to_all(raw, "blk", split_axis=0, concat_axis=2, tiled=True)
    spectra = whiten(regrouped, valid, SEG_LEN, BAND)
    segs = spectra.shape[1]
    bins = SEG_LEN // 2
    table = lag_table(bins, LAGS, SEG_LEN, 1.0 / math.sqrt(bins * segs))
    weight_rows = select[0]
    block = lax.all_gather(spectra, "sub", axis=0, tiled=True)
    stacked = pair_terms(
        block, weight_rows, lax.all_gather(spectra[None], "blk", axis=0, tiled=True)
    )
    return jnp.einsum("injrf,rfl->injl", stacked, table, precision=lax.Precision.HIGHEST)


def solution(mesh):
    return jax.shard_map(
        per_device,
        mesh=mesh,
        in_specs=(
            P("cable", "sub", "blk"),
            P(("cable", "blk"), "sub"),
            P(("cable", "blk"), None, None),
        ),
        out_specs=P(("cable", "blk"), None, "sub", None),
        check_vma=False,
    )
```

profile of v0, /device:TPU:0, one launch (start us, length us, event | category | flops | bytes accessed | tf_op | source)
XLA Modules:
  0.0 73.7 jit_solution(14599562615840998411)
XLA Ops:
  0.0 0.0 copy-start
  0.0 6.4 %all-to-all-start = ((bf16[4,2,1024]{2,1,0:T(2,128)(2,1)}), bf16[4,2,1024]{2,1,0:T(2,128)(2,1)S(1)}, u32[]{:S(2)}, u32[]{:S(2)}) async-start(bf16[4,2,1024]{2,1,0:T(2,128)(2,1)} %param.3), calls=%async_computation | async-start | bytes 32768 | tf_op jit(solution)/shard_map/all_to_all | solution.py:58
  6.5 0.7 convert_bitcast_fusion
  7.1 5.1 %cosine_multiply_fusion = (f32[1,512,512]{2,1,0:T(8,128)S(1)}, f32[1,512,512]{2,1,0:T(8,128)}) fusion(s32[512]{0:T(512)S(1)} %iota_add_fusion, f32[512]{0:T(512)S(1)} %get-tuple-element.17, f32[512]{0:T(512)S(1)} %get-tuple-element.18), kind=kLoop, calls=%fused_computation.35 | loop fusion | flops 4194304 | bytes 2103296 | tf_op jit(solution)/shard_map/mul | solution.py:46
  12.2 0.0 copy-done
  12.2 0.0 all-to-all-done
  12.2 8.6 %fusion.19 = f32[2,4,512]{2,1,0:T(4,128)S(1)} fusion(bf16[4,2,1024]{2,1,0:T(2,128)(2,1)S(1)} %all-to-all-done), kind=kOutput, calls=%fused_computation.29 | convolution fusion | flops 57671680 | bytes 32768 | tf_op jit(solution)/shard_map/cst,tf->csf/dot_general | solution.py:29
  20.8 8.8 %add_reduce_fusion = (f32[2,512]{1,0:T(2,128)S(1)}, f32[2,4,512]{2,1,0:T(4,128)S(1)}) fusion(f32[2,4,512]{2,1,0:T(4,128)S(1)} %fusion.19, bf16[4,2,1024]{2,1,0:T(2,128)(2,1)S(1)} %all-to-all-done), kind=kOutput, calls=%fused_computation.49 | convolution fusion | flops 58211328 | bytes 53248 | tf_op jit(solution)/shard_map/cst,tf->csf/dot_general | solution.py:30
  29.6 0.1 reduce_sum.14
  29.7 0.1 reduce_sum.18
  29.8 0.1 rsqrt_multiply_fusion
  29.9 0.1 mul.169
  29.9 0.1 mul.170
  30.1 13.7 %all_gather.6 = bf16[4,2,4,2,512]{4,2,3,1,0:T(4,128)(2,1)S(1)} all-gather(bf16[1,2,4,2,512]{4,2,3,1,0:T(4,128)(2,1)S(1)} %copy.19), channel_id=1, replica_groups=mesh['cable'=2,'blk'=4,'sub'=4] {'blk'}, dimensions={0}, use_global_device_ids=true | all-gather | bytes 81920 | tf_op jit(solution)/shard_map/all_gather | solution.py:66
  43.8 0.1 multiply_bitcast_fusion
  43.9 1.9 %copy.25 = bf16[4,2,4,2,512,1]{2,0,5,3,1,4:T(4,128)(2,1)S(1)} copy(bf16[4,2,4,2,512,1]{4,2,3,1,0,5:T(4,128)(2,1)S(1)} %multiply_bitcast_fusion) | data formatting | bytes 131072 | tf_op jit(solution)/shard_map/mul | solution.py:50
  45.8 5.4 %all_gather.7 = bf16[8,4,2,512]{3,1,0,2:T(4,128)(2,1)S(1)} all-gather(bf16[2,4,2,512]{3,1,0,2:T(4,128)(2,1)S(1)} %pad_maximum_fusion.1), channel_id=1, replica_groups=mesh['cable'=2,'blk'=4,'sub'=4] {'sub'}, dimensions={0}, use_global_device_ids=true | all-gather | bytes 81920 | tf_op jit(solution)/shard_map/all_gather | solution.py:64
  51.2 2.9 %copy.26 = bf16[8,4,2,512,1,1]{1,0,2,5,4,3:T(8,128)(2,1)} copy(bf16[8,4,2,512,1,1]{3,1,0,2,5,4:T(4,128)(2,1)S(1)} %bitcast.60) | data formatting | bytes 131072 | tf_op jit(solution)/shard_map/all_gather | solution.py:64
  54.2 10.9 %convolution_bitcast_fusion = f32[8,4,2,2,2,512]{0,1,3,4,2,5:T(4,128)S(1)} fusion(bf16[4,2,4,2,512,1]{2,0,5,3,1,4:T(4,128)(2,1)S(1)} %copy.25, bf16[8,4,2,512,1,1]{1,0,2,5,4,3:T(8,128)(2,1)} %copy.26), kind=kOutput, calls=%fused_computation | convolution fusion | flops 1048576 | bytes 655360 | tf_op jit(solution)/shard_map/isaf,njsbf->injabf/dot_general | solution.py:51
  65.0 2.4 %fusion.4 = (f32[8,4,2,1,512]{0,1,2,4,3:T(4,128)}, f32[8,4,2,1,512]{0,1,2,4,3:T(4,128)S(1)}) fusion(f32[8,4,2,2,2,512]{0,1,3,4,2,5:T(4,128)S(1)} %convolution_bitcast_fusion), kind=kLoop, calls=%fused_computation.10 | loop fusion | flops 65536 | bytes 786432 | tf_op jit(solution)/shard_map/add | solution.py:52
  67.5 1.8 %copy.22 = f32[8,4,2,1,512]{4,0,3,2,1:T(8,128)S(1)} copy(f32[8,4,2,1,512]{0,1,2,4,3:T(4,128)} %get-tuple-element.5) | data formatting | bytes 262144 | tf_op jit(solution)/shard_map/add | solution.py:52
  69.3 1.0 %copy.23 = f32[8,4,2,1,512]{4,0,3,2,1:T(8,128)S(1)} copy(f32[8,4,2,1,512]{0,1,2,4,3:T(4,128)S(1)} %get-tuple-element.6) | data formatting | bytes 262144 | tf_op jit(solution)/shard_map/sub | solution.py:53
  70.3 2.6 %fusion.18 = f32[8,4,2,512]{3,0,2,1:T(8,128)S(1)} fusion(f32[1,512,512]{2,1,0:T(8,128)} %get-tuple-element.14, f32[1,512,512]{2,1,0:T(8,128)S(1)} %get-tuple-element.13, f32[8,4,2,1,512]{4,0,3,2,1:T(8,128)S(1)} %copy.23, f32[8,4,2,1,512]{4,0,3,2,1:T(8,128)S(1)} %copy.22), kind=kOutput, calls=%fused_computation.28 | convolution fusion | flops 403243008 | bytes 2490368 | tf_op jit(solution)/shard_map/injrf,rfl->injl/dot_general | solution.py:68
  72.9 0.8 %copy.24 = f32[8,4,2,512]{3,2,1,0:T(2,128)} copy(f32[8,4,2,512]{3,0,2,1:T(8,128)S(1)} %fusion.18) | data formatting | bytes 262144 | tf_op jit(solution)/shard_map/injrf,rfl->injl/dot_general | solution.py:68
  (7 shorter events, 0.1 us)
Async XLA Ops:
  0.0 12.2 %copy-start = (s32[1,2]{1,0:T(1,128)S(1)}, s32[1,2]{1,0:T(1,128)}, u32[]{:S(2)}) copy-start(s32[1,2]{1,0:T(1,128)} %param.4) | copy-start | bytes 28
  0.0 12.2 %all-to-all-start = ((bf16[4,2,1024]{2,1,0:T(2,128)(2,1)}), bf16[4,2,1024]{2,1,0:T(2,128)(2,1)S(1)}, u32[]{:S(2)}, u32[]{:S(2)}) async-start(bf16[4,2,1024]{2,1,0:T(2,128)(2,1)} %param.3), calls=%async_computation | async-start | bytes 32768 | tf_op jit(solution)/shard_map/all_to_all | solution.py:58
where the time goes:
time: 74 us; the launch traced here: 73.7 us
  matrix products  30.9 us (42%)
  blocking collectives  19.1 us (26%)
  local copies, waits for them, and re-layouts  8.68 us (12%)
  other arithmetic  8.5 us (11%)
  starting transfers between devices  6.45 us (9%)
    all_gather x1, blocking collectives, per_device(): lax.all_gather(spectra[None], 'blk', axis=0, tiled=True)  13.7 us
    dot_general x1, matrix products, pair_terms(): jnp.einsum('isaf,njsbf->injabf', own, masked, preferred_element_type=jnp....  10.9 us
    dot_general x1, matrix products, whiten(): jnp.einsum('cst,tf->csf', frames, sin_tab, precision=lax.Precision.HIGHEST)  8.81 us
    dot_general x1, matrix products, whiten(): jnp.einsum('cst,tf->csf', frames, cos_tab, precision=lax.Precision.HIGHEST)  8.58 us
    all_to_all x1, starting transfers between devices, per_device(): lax.all_to_all(raw, 'blk', split_axis=0, concat_axis=2, tiled=True)  6.45 us
    all_gather x1, blocking collectives, per_device(): block = lax.all_gather(spectra, 'sub', axis=0, tiled=True)  5.43 us
    mul x1, other arithmetic, lag_table(): return jnp.stack([weight * jnp.cos(angle), -weight * jnp.sin(angle)])  5.06 us
    all_gather x1, local copies, waits for them, and re-layouts, per_device(): block = lax.all_gather(spectra, 'sub', axis=0, tiled=True)  2.93 us
  transfers between devices with their start and end apart: 1, of which 0 were waited for; matrix products, arithmetic and copies ran while one was open for 8% of the time, Pallas kernels for 0%

commit v1 on v0

--- a/solution.py
+++ b/solution.py
@@ -1,16 +1,230 @@
+import functools
 import math
 
 import jax
 import jax.numpy as jnp
+import numpy as np
 from jax import lax
+from jax.experimental import pallas as pl
+from jax.experimental.pallas import tpu as pltpu
 from jax.sharding import PartitionSpec as P
 
 SEG_LEN = 1024
 BAND = 64
 LAGS = 512
-
+BINS = SEG_LEN // 2
 
 eps = 1e-06
+MESH = pl.DeviceIdType.MESH
+
+
+def split_table(table):
+    high = table.astype(np.float32).astype(jnp.bfloat16)
+    low = (table - high.astype(np.float64)).astype(np.float32).astype(jnp.bfloat16)
+    return np.stack([high, low])
+
+
+def dft_split():
+    times = np.arange(SEG_LEN)[:, None]
+    freqs = np.arange(BINS)[None, :]
+    angle = (times * freqs % SEG_LEN) * (2.0 * math.pi / SEG_LEN)
+    return split_table(np.concatenate([np.cos(angle), -np.sin(angle)], axis=1))
+
+
+def lag_split(scale):
+    freqs = np.arange(BINS)[:, None]
+    shifts = np.arange(LAGS)[None, :] - LAGS // 2
+    angle = (freqs * shifts % SEG_LEN) * (2.0 * math.pi / SEG_LEN)
+    weight = np.where(freqs == 0, 1.0, 2.0) * scale
+    return split_table(
+        np.concatenate([weight * np.cos(angle), -weight * np.sin(angle)], axis=0)
+    )
+
+
+def band_ones():
+    band = np.arange(256) // BAND
+    return (band[:, None] == band[None, :]).astype(jnp.bfloat16)
+
+
+def split(x):
+    high = x.astype(jnp.bfloat16)
+    low = (x - high.astype(jnp.float32)).astype(jnp.bfloat16)
+    return high, low
+
+
+def mxu(a, b):
+    return jnp.dot(a, b, preferred_element_type=jnp.float32)
+
+
+def kernel(
+    nblk, nsub, wide,
+    raw, valid, select, dft, lag, band, out,
+    part, own, vpart, vown, x32, vcol, dft_v, lag_v, band_v,
+    send, recv, vsend, vrecv, local, tabs,
+):
+    me_b, me_u = lax.axis_index("blk"), lax.axis_index("sub")
+    rows = wide * nsub
+    prow = wide * nblk
+    tab_copies = [
+        pltpu.make_async_copy(dft.at[0], dft_v.at[0], tabs.at[0]),
+        pltpu.make_async_copy(dft.at[1], dft_v.at[1], tabs.at[1]),
+        pltpu.make_async_copy(band, band_v, tabs.at[2]),
+        pltpu.make_async_copy(lag, lag_v, tabs.at[3]),
+    ]
+    mine = [
+        pltpu.make_async_copy(raw, part.at[me_b], local.at[0]),
+        pltpu.make_async_copy(valid, vpart.at[me_b], local.at[1]),
+        pltpu.make_async_copy(valid, vown.at[me_u], local.at[2]),
+    ]
+    offsets = [(db, du) for db in range(nblk) for du in range(nsub) if db or du]
+
+    def device(db, du):
+        return {"blk": lax.rem(me_b + db, nblk), "sub": lax.rem(me_u + du, nsub)}
+
+    barrier = pltpu.get_barrier_semaphore()
+    for db, du in offsets:
+        pl.semaphore_signal(
+            barrier, inc=1, device_id=device(db, du), device_id_type=MESH
+        )
+    for copy in mine + tab_copies:
+        copy.start()
+    pl.semaphore_wait(barrier, len(offsets))
+
+    def exchange(db, du, at_b, at_u):
+        there = device(db, du)
+        index = db * nsub + du
+        sems = dict(device_id=there, device_id_type=MESH)
+        copies = []
+        if du == 0:
+            copies.append(pltpu.make_async_remote_copy(
+                raw, part.at[at_b], send.at[index], recv.at[index], **sems))
+            copies.append(pltpu.make_async_remote_copy(
+                valid, vpart.at[at_b], vsend.at[index], vrecv.at[index], **sems))
+        else:
+            copies.append(pltpu.make_async_remote_copy(
+                raw.at[there["blk"]], own.at[at_b, at_u],
+                send.at[index], recv.at[index], **sems))
+            if db == 0:
+                copies.append(pltpu.make_async_remote_copy(
+                    valid, vown.at[at_u], vsend.at[index], vrecv.at[index], **sems))
+        return copies
+
+    order = sorted(offsets, key=lambda o: (o[1] != 0, o))
+    sent, landed = [], []
+    for db, du in order:
+        copies = exchange(db, du, me_b, me_u)
+        for copy in copies:
+            copy.start()
+        sent += copies
+        landed += exchange(
+            db, du, lax.rem(me_b + nblk - db, nblk), lax.rem(me_u + nsub - du, nsub)
+        )
+    for copy in mine:
+        copy.wait()
+    for copy in landed:
+        copy.wait_recv()
+
+    for s in range(nblk):
+        for n in range(nblk):
+            x32[pl.ds(s * prow + n * wide, wide), :] = part[s, n].astype(jnp.float32)
+    base = nblk * prow
+    for s in range(nblk):
+        for u in range(nsub):
+            mine_here = part[s, me_b]
+            piece = jnp.where(me_u == u, mine_here.astype(jnp.float32),
+                              own[s, u].astype(jnp.float32))
+            x32[pl.ds(base + s * rows + u * wide, wide), :] = piece
+    for n in range(nblk):
+        for k in range(wide):
+            vcol[pl.ds(n * wide + k, 1), :] = jnp.broadcast_to(
+                vpart[n][:, k : k + 1].astype(jnp.float32), (1, 128))
+    for u in range(nsub):
+        for k in range(wide):
+            vcol[pl.ds(prow + u * wide + k, 1), :] = jnp.broadcast_to(
+                vown[u][:, k : k + 1].astype(jnp.float32), (1, 128))
+    for copy in tab_copies:
+        copy.wait()
+
+    x = x32[...].astype(jnp.bfloat16)
+    spec = mxu(x, dft_v[0]) + mxu(x, dft_v[1])
+    power = spec[:, :BINS] * spec[:, :BINS] + spec[:, BINS:] * spec[:, BINS:]
+    ppow = sum(power[s * prow : (s + 1) * prow] for s in range(nblk))
+    opow = sum(power[base + s * rows : base + (s + 1) * rows] for s in range(nblk))
+    total = jnp.concatenate([ppow, opow], axis=0)
+    high, low = split(total)
+    both = jnp.concatenate([high, low], axis=0)
+    sums = jnp.concatenate(
+        [mxu(both[:, c : c + 256], band_v[...]) for c in range(0, BINS, 256)], axis=1)
+    level = (sums[: prow + rows] + sums[prow + rows :]) * (1.0 / (BAND * nblk))
+    factor = lax.rsqrt(level + eps) * jnp.tile(vcol[...], (1, BINS // 128))
+    factor = jnp.concatenate([factor, factor], axis=1)
+    fpart, fown = factor[:prow], factor[prow:]
+
+    def rounded(v):
+        return v.astype(jnp.bfloat16).astype(jnp.float32)
+
+    acc_re = [0.0] * rows
+    acc_im = [0.0] * rows
+    row_id = lax.broadcasted_iota(jnp.int32, (prow, 1), 0) // wide
+    for s in range(nblk):
+        b = rounded(spec[s * prow : (s + 1) * prow] * fpart)
+        a = rounded(spec[base + s * rows : base + (s + 1) * rows] * fown)
+        w = jnp.zeros((prow, 1), jnp.float32)
+        for n in range(nblk):
+            w = jnp.where(row_id == n, select[0, n, s].astype(jnp.float32), w)
+        b = b * w
+        br, bi = b[:, :BINS], b[:, BINS:]
+        for i in range(rows):
+            ar, ai = a[i : i + 1, :BINS], a[i : i + 1, BINS:]
+            acc_re[i] = acc_re[i] + (ar * br + ai * bi)
+            acc_im[i] = acc_im[i] + (ai * br - ar * bi)
+    stacked = jnp.concatenate(
+        [jnp.concatenate(acc_re, axis=0), jnp.concatenate(acc_im, axis=0)], axis=1)
+    high, low = split(stacked)
+    count = rows * prow
+    first = mxu(jnp.concatenate([high, low], axis=0), lag_v[0])
+    out[...] = first[:count] + first[count:] + mxu(high, lag_v[1])
+    for copy in sent:
+        copy.wait_send()
+
+
+def fused(nblk, nsub, raw, valid, select):
+    wide = raw.shape[1]
+    rows, prow = wide * nsub, wide * nblk
+    tables = (
+        jnp.asarray(dft_split()),
+        jnp.asarray(lag_split(1.0 / math.sqrt(BINS * nblk))),
+        jnp.asarray(band_ones()),
+    )
+    hbm = pl.BlockSpec(memory_space=pl.ANY)
+    total = nblk * nsub
+    result = pl.pallas_call(
+        functools.partial(kernel, nblk, nsub, wide),
+        out_shape=jax.ShapeDtypeStruct((rows * prow, LAGS), jnp.float32),
+        in_specs=[hbm, hbm, pl.BlockSpec(memory_space=pltpu.SMEM), hbm, hbm, hbm],
+        out_specs=pl.BlockSpec(memory_space=pltpu.VMEM),
+        scratch_shapes=[
+            pltpu.VMEM((nblk, nblk, wide, SEG_LEN), jnp.bfloat16),
+            pltpu.VMEM((nblk, nsub, wide, SEG_LEN), jnp.bfloat16),
+            pltpu.VMEM((nblk, 1, wide), jnp.int32),
+            pltpu.VMEM((nsub, 1, wide), jnp.int32),
+            pltpu.VMEM((nblk * (rows + prow), SEG_LEN), jnp.float32),
+            pltpu.VMEM((rows + prow, 128), jnp.float32),
+            pltpu.VMEM((2, SEG_LEN, 2 * BINS), jnp.bfloat16),
+            pltpu.VMEM((2, 2 * BINS, LAGS), jnp.bfloat16),
+            pltpu.VMEM((256, 256), jnp.bfloat16),
+            pltpu.SemaphoreType.DMA((total,)),
+            pltpu.SemaphoreType.DMA((total,)),
+            pltpu.SemaphoreType.DMA((total,)),
+            pltpu.SemaphoreType.DMA((total,)),
+            pltpu.SemaphoreType.DMA((3,)),
+            pltpu.SemaphoreType.DMA((4,)),
+        ],
+        compiler_params=pltpu.CompilerParams(
+            collective_id=0, has_side_effects=True, vmem_limit_bytes=32 * 2**20
+        ),
+    )(raw, valid, select, *tables)
+    return result.reshape(rows, nblk, wide, LAGS)
 
 
 def dft_tables(length, bins):
@@ -54,21 +268,27 @@
     return jnp.stack([real, imag], axis=3)
 
 
-def per_device(raw, valid, select):
+def by_collectives(raw, valid, select):
     regrouped = lax.all_to_all(raw, "blk", split_axis=0, concat_axis=2, tiled=True)
     spectra = whiten(regrouped, valid, SEG_LEN, BAND)
     segs = spectra.shape[1]
-    bins = SEG_LEN // 2
-    table = lag_table(bins, LAGS, SEG_LEN, 1.0 / math.sqrt(bins * segs))
-    weight_rows = select[0]
+    table = lag_table(BINS, LAGS, SEG_LEN, 1.0 / math.sqrt(BINS * segs))
     block = lax.all_gather(spectra, "sub", axis=0, tiled=True)
     stacked = pair_terms(
-        block, weight_rows, lax.all_gather(spectra[None], "blk", axis=0, tiled=True)
+        block, select[0], lax.all_gather(spectra[None], "blk", axis=0, tiled=True)
     )
     return jnp.einsum("injrf,rfl->injl", stacked, table, precision=lax.Precision.HIGHEST)
 
 
 def solution(mesh):
+    nblk, nsub = mesh.shape["blk"], mesh.shape["sub"]
+
+    def per_device(raw, valid, select):
+        fits = raw.shape[2] == SEG_LEN and raw.shape[0] == nblk and nblk * nsub <= 16
+        if fits:
+            return fused(nblk, nsub, raw, valid, select)
+        return by_collectives(raw, valid, select)
+
     return jax.shard_map(
         per_device,
         mesh=mesh,

time: 74 us -> 20.6 us (0.28)
  matrix products: 30.9 us -> 0 us
  blocking collectives: 19.1 us -> 0 us
  Pallas kernels: 0 us -> 12.8 us
  other arithmetic: 8.5 us -> 0 us
  starting transfers between devices: 6.45 us -> 0 us
  local copies, waits for them, and re-layouts: 8.68 us -> 7.46 us
    dot_general x4 -> x0, matrix products: 30.9 us -> none  [the longest x1 10.9 us: pair_terms(): jnp.einsum('isaf,njsbf->injabf', own, masked, preferred_element_type=jnp....]
    all_gather x2 -> x0, blocking collectives: 19.1 us -> none  [the longest x1 13.7 us: per_device(): lax.all_gather(spectra[None], 'blk', axis=0, tiled=True)]
    pallas_call x0 -> x1, Pallas kernels: none -> 12.8 us  [fused(): pl.pallas_call(functools.partial(kernel, nblk, nsub, wide), out_shape=jax...]
    unnamed x2 -> x12, local copies, waits for them, and re-layouts: 0.01 us -> 6.73 us
    all_to_all x1 -> x0, starting transfers between devices: 6.45 us -> none  [per_device(): lax.all_to_all(raw, 'blk', split_axis=0, concat_axis=2, tiled=True)]
    mul x4 -> x0, other arithmetic: 5.18 us -> none  [the longest x1 5.06 us: lag_table(): return jnp.stack([weight * jnp.cos(angle), -weight * jnp.sin(angle)])]
    all_gather x1 -> x0, local copies, waits for them, and re-layouts: 2.93 us -> none  [per_device(): block = lax.all_gather(spectra, 'sub', axis=0, tiled=True)]
    add x1 -> x0, other arithmetic: 2.43 us -> none  [pair_terms(): real = prod[:, :, :, 0, 0] + prod[:, :, :, 1, 1]]
  transfers between devices with their start and end apart: 1 -> 0, of which waited for: 0 -> 0; matrix products, arithmetic and copies ran while one was open for 8% -> 0% of each run, Pallas kernels for 0% -> 0%
where the time goes in v1:
time: 20.6 us; the launch traced here: 20.3 us
  Pallas kernels  12.8 us (62%)
  local copies, waits for them, and re-layouts  7.46 us (36%)
    pallas_call x1, Pallas kernels, fused(): pl.pallas_call(functools.partial(kernel, nblk, nsub, wide), out_shape=jax...  12.8 us
    unnamed x12, local copies, waits for them, and re-layouts  6.73 us
    reshape x1, local copies, waits for them, and re-layouts, fused(): return result.reshape(rows, nblk, wide, LAGS)  0.73 us

profile of v1, /device:TPU:0, one launch (start us, length us, event | category | flops | bytes accessed | tf_op | source)
XLA Modules:
  0.0 20.3 jit_solution(1051801443327070657)
XLA Ops:
  0.0 0.0 copy-start
  0.0 2.2 %copy-done = bf16[2,1024,1024]{2,1,0:T(8,128)(2,1)S(1)} copy-done((bf16[2,1024,1024]{2,1,0:T(8,128)(2,1)S(1)}, bf16[2,1024,1024]{2,1,0:T(8,128)(2,1)}, u32[]{:S(2)}) %copy-start) | copy-done | bytes 4194328
  2.2 0.0 copy-start.1
  2.2 1.6 %copy-done.1 = bf16[2,1024,512]{2,1,0:T(8,128)(2,1)S(1)} copy-done((bf16[2,1024,512]{2,1,0:T(8,128)(2,1)S(1)}, bf16[2,1024,512]{2,1,0:T(8,128)(2,1)}, u32[]{:S(2)}) %copy-start.1) | copy-done | bytes 2097176
  3.8 0.0 copy-start.2
  3.8 0.9 %copy-done.2 = bf16[256,256]{1,0:T(8,128)(2,1)S(1)} copy-done((bf16[256,256]{1,0:T(8,128)(2,1)S(1)}, bf16[256,256]{1,0:T(8,128)(2,1)}, u32[]{:S(2)}) %copy-start.2) | copy-done | bytes 131096
  4.7 0.0 copy-start.3
  4.7 0.7 %copy-done.3 = bf16[4,2,1024]{2,1,0:T(2,128)(2,1)S(1)} copy-done((bf16[4,2,1024]{2,1,0:T(2,128)(2,1)S(1)}, bf16[4,2,1024]{2,1,0:T(2,128)(2,1)}, u32[]{:S(2)}) %copy-start.3) | copy-done | bytes 16408
  5.4 0.0 copy-start.4
  5.4 0.7 %copy-done.4 = s32[1,4,4]{2,1,0:T(4,128)S(1)} copy-done((s32[1,4,4]{2,1,0:T(4,128)S(1)}, s32[1,4,4]{2,1,0:T(4,128)}, u32[]{:S(2)}) %copy-start.4) | copy-done | bytes 88
  6.1 0.0 copy-start.5
  6.1 0.7 %copy-done.5 = s32[1,2]{1,0:T(1,128)S(1)} copy-done((s32[1,2]{1,0:T(1,128)S(1)}, s32[1,2]{1,0:T(1,128)}, u32[]{:S(2)}) %copy-start.5) | copy-done | bytes 32
  6.7 12.8 %shard_map.64 = f32[64,512]{1,0:T(8,128)S(1)} custom-call(bf16[4,2,1024]{2,1,0:T(2,128)(2,1)S(1)} %copy-done.3, s32[1,2]{1,0:T(1,128)S(1)} %copy-done.5, s32[1,4,4]{2,1,0:T(4,128)S(1)} %copy-done.4, bf16[2,1024,1024]{2,1,0:T(8,128)(2,1)S(1)} %copy-done, bf16[2,1024,512]{2,1,0:T(8,128)(2,1)S(1)} %copy-done.1, bf16[256,256]{1,0:T(8,128)(2,1)S(1)} %copy-done.2), custom_call_target="tpu_custom_call" | custom-call | tf_op jit(solution)/shard_map/pallas_call | solution.py:201
  19.5 0.7 %reshape.3 = f32[8,4,2,512]{3,2,1,0:T(2,128)} reshape(f32[64,512]{1,0:T(8,128)S(1)} %shard_map.64) | data formatting | bytes 262144 | tf_op jit(solution)/shard_map/reshape | solution.py:227
Async XLA Ops:
  0.0 2.2 %copy-start = (bf16[2,1024,1024]{2,1,0:T(8,128)(2,1)S(1)}, bf16[2,1024,1024]{2,1,0:T(8,128)(2,1)}, u32[]{:S(2)}) copy-start(bf16[2,1024,1024]{2,1,0:T(8,128)(2,1)} %constant.6.clone.dft) | copy-start | bytes 12582916
  2.2 1.6 %copy-start.1 = (bf16[2,1024,512]{2,1,0:T(8,128)(2,1)S(1)}, bf16[2,1024,512]{2,1,0:T(8,128)(2,1)}, u32[]{:S(2)}) copy-start(bf16[2,1024,512]{2,1,0:T(8,128)(2,1)} %constant.7.clone.lag) | copy-start | bytes 6291460
  3.8 0.9 %copy-start.2 = (bf16[256,256]{1,0:T(8,128)(2,1)S(1)}, bf16[256,256]{1,0:T(8,128)(2,1)}, u32[]{:S(2)}) copy-start(bf16[256,256]{1,0:T(8,128)(2,1)} %constant.8.clone.band) | copy-start | bytes 393220
  4.7 0.7 %copy-start.3 = (bf16[4,2,1024]{2,1,0:T(2,128)(2,1)S(1)}, bf16[4,2,1024]{2,1,0:T(2,128)(2,1)}, u32[]{:S(2)}) copy-start(bf16[4,2,1024]{2,1,0:T(2,128)(2,1)} %raw.1) | copy-start | bytes 49156
  5.4 0.7 %copy-start.4 = (s32[1,4,4]{2,1,0:T(4,128)S(1)}, s32[1,4,4]{2,1,0:T(4,128)}, u32[]{:S(2)}) copy-start(s32[1,4,4]{2,1,0:T(4,128)} %select.1) | copy-start | bytes 196
  6.1 0.7 %copy-start.5 = (s32[1,2]{1,0:T(1,128)S(1)}, s32[1,2]{1,0:T(1,128)}, u32[]{:S(2)}) copy-start(s32[1,2]{1,0:T(1,128)} %valid.1) | copy-start | bytes 28

commit v2 on v1

--- a/solution.py
+++ b/solution.py
@@ -58,8 +58,8 @@
 
 def kernel(
     nblk, nsub, wide,
-    raw, valid, select, dft, lag, band, out,
-    part, own, vpart, vown, x32, vcol, dft_v, lag_v, band_v,
+    raw, valid, choose, dft, lag, band, out,
+    select, part, own, vpart, vown, x32, vcol, dft_v, lag_v, band_v,
     send, recv, vsend, vrecv, local, tabs,
 ):
     me_b, me_u = lax.axis_index("blk"), lax.axis_index("sub")
@@ -75,6 +75,7 @@
         pltpu.make_async_copy(raw, part.at[me_b], local.at[0]),
         pltpu.make_async_copy(valid, vpart.at[me_b], local.at[1]),
         pltpu.make_async_copy(valid, vown.at[me_u], local.at[2]),
+        pltpu.make_async_copy(choose, select, local.at[3]),
     ]
     offsets = [(db, du) for db in range(nblk) for du in range(nsub) if db or du]
 
@@ -196,14 +197,15 @@
         jnp.asarray(lag_split(1.0 / math.sqrt(BINS * nblk))),
         jnp.asarray(band_ones()),
     )
-    hbm = pl.BlockSpec(memory_space=pl.ANY)
+    hbm = pl.BlockSpec(memory_space=pltpu.HBM)
     total = nblk * nsub
     result = pl.pallas_call(
         functools.partial(kernel, nblk, nsub, wide),
         out_shape=jax.ShapeDtypeStruct((rows * prow, LAGS), jnp.float32),
-        in_specs=[hbm, hbm, pl.BlockSpec(memory_space=pltpu.SMEM), hbm, hbm, hbm],
+        in_specs=[hbm] * 6,
         out_specs=pl.BlockSpec(memory_space=pltpu.VMEM),
         scratch_shapes=[
+            pltpu.SMEM(select.shape, jnp.int32),
             pltpu.VMEM((nblk, nblk, wide, SEG_LEN), jnp.bfloat16),
             pltpu.VMEM((nblk, nsub, wide, SEG_LEN), jnp.bfloat16),
             pltpu.VMEM((nblk, 1, wide), jnp.int32),
@@ -217,7 +219,7 @@
             pltpu.SemaphoreType.DMA((total,)),
             pltpu.SemaphoreType.DMA((total,)),
             pltpu.SemaphoreType.DMA((total,)),
-            pltpu.SemaphoreType.DMA((3,)),
+            pltpu.SemaphoreType.DMA((4,)),
             pltpu.SemaphoreType.DMA((4,)),
         ],
         compiler_params=pltpu.CompilerParams(

time: 20.6 us -> 20 us (0.971)
  Pallas kernels: 12.8 us -> 12.2 us
    pallas_call x1, Pallas kernels: 12.8 us -> 12.2 us  [fused(): pl.pallas_call(functools.partial(kernel, nblk, nsub, wide), out_shape=jax...]
where the time goes in v2:
time: 20 us; the launch traced here: 19.7 us
  Pallas kernels  12.2 us (61%)
  local copies, waits for them, and re-layouts  7.46 us (37%)
    pallas_call x1, Pallas kernels, fused(): pl.pallas_call(functools.partial(kernel, nblk, nsub, wide), out_shape=jax...  12.2 us
    unnamed x12, local copies, waits for them, and re-layouts  6.73 us
    reshape x1, local copies, waits for them, and re-layouts, fused(): return result.reshape(rows, nblk, wide, LAGS)  0.73 us

profile of v2, /device:TPU:0, one launch (start us, length us, event | category | flops | bytes accessed | tf_op | source)
XLA Modules:
  0.0 19.7 jit_solution(4799311632384725205)
XLA Ops:
  0.0 0.0 copy-start
  0.0 2.2 %copy-done = bf16[2,1024,1024]{2,1,0:T(8,128)(2,1)S(1)} copy-done((bf16[2,1024,1024]{2,1,0:T(8,128)(2,1)S(1)}, bf16[2,1024,1024]{2,1,0:T(8,128)(2,1)}, u32[]{:S(2)}) %copy-start) | copy-done | bytes 4194328
  2.2 0.0 copy-start.1
  2.2 1.6 %copy-done.1 = bf16[2,1024,512]{2,1,0:T(8,128)(2,1)S(1)} copy-done((bf16[2,1024,512]{2,1,0:T(8,128)(2,1)S(1)}, bf16[2,1024,512]{2,1,0:T(8,128)(2,1)}, u32[]{:S(2)}) %copy-start.1) | copy-done | bytes 2097176
  3.8 0.0 copy-start.2
  3.8 0.9 %copy-done.2 = bf16[256,256]{1,0:T(8,128)(2,1)S(1)} copy-done((bf16[256,256]{1,0:T(8,128)(2,1)S(1)}, bf16[256,256]{1,0:T(8,128)(2,1)}, u32[]{:S(2)}) %copy-start.2) | copy-done | bytes 131096
  4.7 0.0 copy-start.3
  4.7 0.7 %copy-done.3 = bf16[4,2,1024]{2,1,0:T(2,128)(2,1)S(1)} copy-done((bf16[4,2,1024]{2,1,0:T(2,128)(2,1)S(1)}, bf16[4,2,1024]{2,1,0:T(2,128)(2,1)}, u32[]{:S(2)}) %copy-start.3) | copy-done | bytes 16408
  5.4 0.0 copy-start.4
  5.4 0.7 %copy-done.4 = s32[1,4,4]{2,1,0:T(4,128)S(1)} copy-done((s32[1,4,4]{2,1,0:T(4,128)S(1)}, s32[1,4,4]{2,1,0:T(4,128)}, u32[]{:S(2)}) %copy-start.4) | copy-done | bytes 88
  6.1 0.0 copy-start.5
  6.1 0.7 %copy-done.5 = s32[1,2]{1,0:T(1,128)S(1)} copy-done((s32[1,2]{1,0:T(1,128)S(1)}, s32[1,2]{1,0:T(1,128)}, u32[]{:S(2)}) %copy-start.5) | copy-done | bytes 32
  6.7 12.2 %shard_map.64 = f32[64,512]{1,0:T(8,128)S(1)} custom-call(bf16[4,2,1024]{2,1,0:T(2,128)(2,1)S(1)} %copy-done.3, s32[1,2]{1,0:T(1,128)S(1)} %copy-done.5, s32[1,4,4]{2,1,0:T(4,128)S(1)} %copy-done.4, bf16[2,1024,1024]{2,1,0:T(8,128)(2,1)S(1)} %copy-done, bf16[2,1024,512]{2,1,0:T(8,128)(2,1)S(1)} %copy-done.1, bf16[256,256]{1,0:T(8,128)(2,1)S(1)} %copy-done.2), custom_call_target="tpu_custom_call" | custom-call | tf_op jit(solution)/shard_map/pallas_call | solution.py:202
  19.0 0.7 %reshape.3 = f32[8,4,2,512]{3,2,1,0:T(2,128)} reshape(f32[64,512]{1,0:T(8,128)S(1)} %shard_map.64) | data formatting | bytes 262144 | tf_op jit(solution)/shard_map/reshape | solution.py:229
Async XLA Ops:
  0.0 2.2 %copy-start = (bf16[2,1024,1024]{2,1,0:T(8,128)(2,1)S(1)}, bf16[2,1024,1024]{2,1,0:T(8,128)(2,1)}, u32[]{:S(2)}) copy-start(bf16[2,1024,1024]{2,1,0:T(8,128)(2,1)} %constant.6.clone.dft) | copy-start | bytes 12582916
  2.2 1.6 %copy-start.1 = (bf16[2,1024,512]{2,1,0:T(8,128)(2,1)S(1)}, bf16[2,1024,512]{2,1,0:T(8,128)(2,1)}, u32[]{:S(2)}) copy-start(bf16[2,1024,512]{2,1,0:T(8,128)(2,1)} %constant.7.clone.lag) | copy-start | bytes 6291460
  3.8 0.9 %copy-start.2 = (bf16[256,256]{1,0:T(8,128)(2,1)S(1)}, bf16[256,256]{1,0:T(8,128)(2,1)}, u32[]{:S(2)}) copy-start(bf16[256,256]{1,0:T(8,128)(2,1)} %constant.8.clone.band) | copy-start | bytes 393220
  4.7 0.7 %copy-start.3 = (bf16[4,2,1024]{2,1,0:T(2,128)(2,1)S(1)}, bf16[4,2,1024]{2,1,0:T(2,128)(2,1)}, u32[]{:S(2)}) copy-start(bf16[4,2,1024]{2,1,0:T(2,128)(2,1)} %raw.1) | copy-start | bytes 49156
  5.4 0.7 %copy-start.4 = (s32[1,4,4]{2,1,0:T(4,128)S(1)}, s32[1,4,4]{2,1,0:T(4,128)}, u32[]{:S(2)}) copy-start(s32[1,4,4]{2,1,0:T(4,128)} %choose.1) | copy-start | bytes 196
  6.1 0.7 %copy-start.5 = (s32[1,2]{1,0:T(1,128)S(1)}, s32[1,2]{1,0:T(1,128)}, u32[]{:S(2)}) copy-start(s32[1,2]{1,0:T(1,128)} %valid.1) | copy-start | bytes 28

commit v3 on v2

--- a/solution.py
+++ b/solution.py
@@ -42,8 +42,9 @@
 
 
 def band_ones():
-    band = np.arange(256) // BAND
-    return (band[:, None] == band[None, :]).astype(jnp.bfloat16)
+    first = lax.broadcasted_iota(jnp.int32, (256, 256), 0) // BAND
+    second = lax.broadcasted_iota(jnp.int32, (256, 256), 1) // BAND
+    return jnp.where(first == second, 1.0, 0.0).astype(jnp.bfloat16)
 
 
 def split(x):
@@ -58,8 +59,8 @@
 
 def kernel(
     nblk, nsub, wide,
-    raw, valid, choose, dft, lag, band, out,
-    select, part, own, vpart, vown, x32, vcol, dft_v, lag_v, band_v,
+    raw, valid, choose, dft, lag, out,
+    select, part, own, vpart, vown, x32, vcol, dft_v, lag_v,
     send, recv, vsend, vrecv, local, tabs,
 ):
     me_b, me_u = lax.axis_index("blk"), lax.axis_index("sub")
@@ -68,8 +69,7 @@
     tab_copies = [
         pltpu.make_async_copy(dft.at[0], dft_v.at[0], tabs.at[0]),
         pltpu.make_async_copy(dft.at[1], dft_v.at[1], tabs.at[1]),
-        pltpu.make_async_copy(band, band_v, tabs.at[2]),
-        pltpu.make_async_copy(lag, lag_v, tabs.at[3]),
+        pltpu.make_async_copy(lag, lag_v, tabs.at[2]),
     ]
     mine = [
         pltpu.make_async_copy(raw, part.at[me_b], local.at[0]),
@@ -87,8 +87,6 @@
         pl.semaphore_signal(
             barrier, inc=1, device_id=device(db, du), device_id_type=MESH
         )
-    for copy in mine + tab_copies:
-        copy.start()
     pl.semaphore_wait(barrier, len(offsets))
 
     def exchange(db, du, at_b, at_u):
@@ -120,6 +118,8 @@
         landed += exchange(
             db, du, lax.rem(me_b + nblk - db, nblk), lax.rem(me_u + nsub - du, nsub)
         )
+    for copy in mine + tab_copies:
+        copy.start()
     for copy in mine:
         copy.wait()
     for copy in landed:
@@ -152,10 +152,11 @@
     ppow = sum(power[s * prow : (s + 1) * prow] for s in range(nblk))
     opow = sum(power[base + s * rows : base + (s + 1) * rows] for s in range(nblk))
     total = jnp.concatenate([ppow, opow], axis=0)
+    ones = band_ones()
     high, low = split(total)
     both = jnp.concatenate([high, low], axis=0)
     sums = jnp.concatenate(
-        [mxu(both[:, c : c + 256], band_v[...]) for c in range(0, BINS, 256)], axis=1)
+        [mxu(both[:, c : c + 256], ones) for c in range(0, BINS, 256)], axis=1)
     level = (sums[: prow + rows] + sums[prow + rows :]) * (1.0 / (BAND * nblk))
     factor = lax.rsqrt(level + eps) * jnp.tile(vcol[...], (1, BINS // 128))
     factor = jnp.concatenate([factor, factor], axis=1)
@@ -195,14 +196,13 @@
     tables = (
         jnp.asarray(dft_split()),
         jnp.asarray(lag_split(1.0 / math.sqrt(BINS * nblk))),
-        jnp.asarray(band_ones()),
     )
     hbm = pl.BlockSpec(memory_space=pltpu.HBM)
     total = nblk * nsub
     result = pl.pallas_call(
         functools.partial(kernel, nblk, nsub, wide),
         out_shape=jax.ShapeDtypeStruct((rows * prow, LAGS), jnp.float32),
-        in_specs=[hbm] * 6,
+        in_specs=[hbm] * 5,
         out_specs=pl.BlockSpec(memory_space=pltpu.VMEM),
         scratch_shapes=[
             pltpu.SMEM(select.shape, jnp.int32),
@@ -214,18 +214,17 @@
             pltpu.VMEM((rows + prow, 128), jnp.float32),
             pltpu.VMEM((2, SEG_LEN, 2 * BINS), jnp.bfloat16),
             pltpu.VMEM((2, 2 * BINS, LAGS), jnp.bfloat16),
-            pltpu.VMEM((256, 256), jnp.bfloat16),
             pltpu.SemaphoreType.DMA((total,)),
             pltpu.SemaphoreType.DMA((total,)),
             pltpu.SemaphoreType.DMA((total,)),
             pltpu.SemaphoreType.DMA((total,)),
             pltpu.SemaphoreType.DMA((4,)),
-            pltpu.SemaphoreType.DMA((4,)),
+            pltpu.SemaphoreType.DMA((3,)),
         ],
         compiler_params=pltpu.CompilerParams(
             collective_id=0, has_side_effects=True, vmem_limit_bytes=32 * 2**20
         ),
-    )(raw, valid, select, *tables)
+    )(*(pltpu.with_memory_space_constraint(a, pltpu.HBM) for a in (raw, valid, select) + tables))
     return result.reshape(rows, nblk, wide, LAGS)
 
 

time: 20 us -> 13.4 us (0.67)
  local copies, waits for them, and re-layouts: 7.46 us -> 0.73 us
  Pallas kernels: 12.2 us -> 12.4 us
    unnamed x12 -> x0, local copies, waits for them, and re-layouts: 6.73 us -> none
    pallas_call x1, Pallas kernels: 12.2 us -> 12.4 us  [fused(): pl.pallas_call(functools.partial(kernel, nblk, nsub, wide), out_shape=jax...]
where the time goes in v3:
time: 13.4 us; the launch traced here: 13.2 us
  Pallas kernels  12.4 us (93%)
  local copies, waits for them, and re-layouts  0.73 us (5%)
    pallas_call x1, Pallas kernels, fused(): pl.pallas_call(functools.partial(kernel, nblk, nsub, wide), out_shape=jax...  12.4 us
    reshape x1, local copies, waits for them, and re-layouts, fused(): return result.reshape(rows, nblk, wide, LAGS)  0.73 us

profile of v3, /device:TPU:0, one launch (start us, length us, event | category | flops | bytes accessed | tf_op | source)
XLA Modules:
  0.0 13.2 jit_solution(2773843731889038927)
XLA Ops:
  0.0 12.4 %shard_map.55 = f32[64,512]{1,0:T(8,128)S(1)} custom-call(bf16[4,2,1024]{2,1,0:T(2,128)(2,1)} %raw.1, s32[1,2]{1,0:T(1,128)} %valid.1, s32[1,4,4]{2,1,0:T(4,128)} %choose.1, bf16[2,1024,1024]{2,1,0:T(8,128)(2,1)} %constant.4.clone.dft, bf16[2,1024,512]{2,1,0:T(8,128)(2,1)} %constant.5.clone.lag), custom_call_target="tpu_custom_call" | custom-call | tf_op jit(solution)/shard_map/pallas_call | solution.py:202
  12.4 0.7 %reshape.3 = f32[8,4,2,512]{3,2,1,0:T(2,128)} reshape(f32[64,512]{1,0:T(8,128)S(1)} %shard_map.55) | data formatting | bytes 262144 | tf_op jit(solution)/shard_map/reshape | solution.py:228

commit v4 on v0

--- a/solution.py
+++ b/solution.py
@@ -1,16 +1,295 @@
+import functools
 import math
 
 import jax
 import jax.numpy as jnp
+import numpy as np
 from jax import lax
+from jax.experimental import pallas as pl
+from jax.experimental.pallas import tpu as pltpu
 from jax.sharding import PartitionSpec as P
 
 SEG_LEN = 1024
 BAND = 64
 LAGS = 512
-
+BINS = SEG_LEN // 2
+QUARTER = SEG_LEN // 4
+GROUP = BINS // 4
 
 eps = 1e-06
+MESH = pl.DeviceIdType.MESH
+
+
+def split_table(table):
+    high = table.astype(np.float32).astype(jnp.bfloat16)
+    low = (table - high.astype(np.float64)).astype(np.float32).astype(jnp.bfloat16)
+    return np.stack([high, low])
+
+
+def waves(freqs, times):
+    angle = (freqs * times % SEG_LEN) * (2.0 * math.pi / SEG_LEN)
+    return np.cos(angle), -np.sin(angle)
+
+
+def bins_of(*classes):
+    return np.concatenate([np.arange(r, BINS, 4) for r in classes])
+
+
+def dft_split():
+    def table(length, *classes):
+        freqs = bins_of(*classes)[None, :]
+        return np.concatenate(waves(freqs, np.arange(length)[:, None]), axis=1)
+
+    even = np.concatenate([table(QUARTER, 0), table(QUARTER, 2)], axis=1)
+    return split_table(np.concatenate([even, table(2 * QUARTER, 1, 3)], axis=0))
+
+
+def lag_split(scale):
+    def table(count, *classes):
+        freqs = bins_of(*classes)[:, None]
+        weight = np.where(freqs == 0, 1.0, 2.0) * scale
+        shifts = np.arange(count)[None, :] - LAGS // 2
+        return np.concatenate([weight * w for w in waves(freqs, shifts)], axis=0)
+
+    even = np.concatenate([table(LAGS // 2, 0), table(LAGS // 2, 2)], axis=1)
+    return split_table(np.concatenate([even, table(LAGS, 1, 3)], axis=0))
+
+
+def band_ones():
+    width = BAND // 4
+    first = lax.broadcasted_iota(jnp.int32, (GROUP, GROUP), 0) // width
+    second = lax.broadcasted_iota(jnp.int32, (GROUP, GROUP), 1) // width
+    return jnp.where(first == second, 1.0, 0.0).astype(jnp.bfloat16)
+
+
+def split(x):
+    high = x.astype(jnp.bfloat16)
+    low = (x - high.astype(jnp.float32)).astype(jnp.bfloat16)
+    return high, low
+
+
+def mxu(a, b):
+    return jnp.dot(a, b, preferred_element_type=jnp.float32)
+
+
+def rounded(v):
+    return v.astype(jnp.bfloat16).astype(jnp.float32)
+
+
+def groups(v):
+    return [v[:, c : c + GROUP] for c in range(0, v.shape[1], GROUP)]
+
+
+def wide_mxu(v, table, rows, cols):
+    high, low = split(v)
+    count = v.shape[0]
+    first = mxu(jnp.concatenate([high, low], axis=0), table[0, rows, cols])
+    return first[:count] + first[count:] + mxu(high, table[1, rows, cols])
+
+
+EVEN, ODD = slice(0, QUARTER), slice(QUARTER, 3 * QUARTER)
+LEFT, RIGHT, ALL = slice(0, QUARTER), slice(QUARTER, 2 * QUARTER), slice(None)
+
+
+def spectrum(x, table):
+    q = [x[:, c : c + QUARTER] for c in range(0, SEG_LEN, QUARTER)]
+    plus, cross = q[0] + q[2], q[1] + q[3]
+    zero = wide_mxu(plus + cross, table, EVEN, LEFT)
+    two = wide_mxu(plus - cross, table, EVEN, RIGHT)
+    odd = wide_mxu(
+        jnp.concatenate([q[0] - q[2], q[1] - q[3]], axis=1), table, ODD, ALL)
+    real = [zero[:, :GROUP], two[:, :GROUP], odd[:, : 2 * GROUP]]
+    imag = [zero[:, GROUP:], two[:, GROUP:], odd[:, 2 * GROUP :]]
+    return jnp.concatenate(real + imag, axis=1)
+
+
+def lags_of(v, table):
+    g = groups(v)
+    zero = wide_mxu(jnp.concatenate([g[0], g[4]], axis=1), table, EVEN, LEFT)
+    two = wide_mxu(jnp.concatenate([g[1], g[5]], axis=1), table, EVEN, RIGHT)
+    odd = wide_mxu(
+        jnp.concatenate([g[2], g[3], g[6], g[7]], axis=1), table, ODD, ALL)
+    return jnp.concatenate([zero + two, zero - two], axis=1) + odd
+
+
+def kernel(
+    nblk, nsub, wide,
+    raw, valid, choose, dft, lag, out,
+    select, part, own, vpart, vown, x32, vcol, dft_v, lag_v,
+    send, recv, vsend, vrecv, fsend, frecv, local, tabs,
+):
+    me_b, me_u = lax.axis_index("blk"), lax.axis_index("sub")
+    rows = wide * nsub
+    prow = wide * nblk
+    blks, subs = range(1, nblk), range(1, nsub)
+
+    def at_blk(db):
+        return {"blk": lax.rem(me_b + db, nblk)}
+
+    def at_sub(du):
+        return {"sub": lax.rem(me_u + du, nsub)}
+
+    tab_copies = [
+        pltpu.make_async_copy(dft, dft_v, tabs.at[0]),
+        pltpu.make_async_copy(lag, lag_v, tabs.at[1]),
+    ]
+    mine = [
+        pltpu.make_async_copy(raw, part.at[0], local.at[0]),
+        pltpu.make_async_copy(valid, vpart.at[me_b], local.at[1]),
+        pltpu.make_async_copy(valid, vown.at[me_u], local.at[2]),
+        pltpu.make_async_copy(choose, select, local.at[3]),
+        pltpu.make_async_copy(raw.at[me_b], own.at[0, me_u], local.at[4]),
+    ]
+
+    barrier = pltpu.get_barrier_semaphore()
+    order = list(blks)
+    others = [(db, du) for db in range(nblk) for du in range(nsub) if db or du]
+    for db, du in others:
+        pl.semaphore_signal(
+            barrier, inc=1, device_id={**at_blk(db), **at_sub(du)}, device_id_type=MESH)
+    for copy in mine:
+        copy.start()
+    pl.semaphore_wait(barrier, len(others))
+
+    def samples(db):
+        return pltpu.make_async_remote_copy(
+            raw, part.at[db], send.at[db], recv.at[db],
+            device_id=at_blk(db), device_id_type=MESH)
+
+    def valid_blk(db, at_b):
+        return pltpu.make_async_remote_copy(
+            valid, vpart.at[at_b], vsend.at[db], vrecv.at[db],
+            device_id=at_blk(db), device_id_type=MESH)
+
+    def valid_sub(du, at_u):
+        return pltpu.make_async_remote_copy(
+            valid, vown.at[at_u], vsend.at[nblk + du], vrecv.at[nblk + du],
+            device_id=at_sub(du), device_id_type=MESH)
+
+    def block(db, du, at_u):
+        there = at_blk(db)
+        return pltpu.make_async_remote_copy(
+            raw.at[there["blk"]], own.at[db, at_u], fsend.at[db, du], frecv.at[db, du],
+            device_id={**there, **at_sub(du)}, device_id_type=MESH)
+
+    sent = [samples(db) for db in order]
+    sent += [valid_blk(db, me_b) for db in order]
+    sent += [valid_sub(du, me_u) for du in subs]
+    sent += [block(db, du, me_u) for db in range(nblk) for du in subs]
+    for copy in sent + tab_copies:
+        copy.start()
+
+    def place(ref, base, count):
+        for c in range(count):
+            x32[pl.ds(base + c * wide, wide), :] = ref[c].astype(jnp.float32)
+
+    base = nblk * prow
+    for copy in mine:
+        copy.wait()
+    place(part.at[0], 0, nblk)
+    moved = []
+    for db in order:
+        samples(db).wait_recv()
+        keep = pltpu.make_async_copy(
+            part.at[db, me_b], own.at[db, me_u], fsend.at[db, 0])
+        keep.start()
+        moved.append(keep)
+        place(part.at[db], db * prow, nblk)
+
+    for db in blks:
+        valid_blk(db, lax.rem(me_b + nblk - db, nblk)).wait_recv()
+    for du in subs:
+        valid_sub(du, lax.rem(me_u + nsub - du, nsub)).wait_recv()
+    for n in range(nblk):
+        for k in range(wide):
+            vcol[pl.ds(n * wide + k, 1), :] = jnp.broadcast_to(
+                vpart[n][:, k : k + 1].astype(jnp.float32), (1, 128))
+    for u in range(nsub):
+        for k in range(wide):
+            vcol[pl.ds(prow + u * wide + k, 1), :] = jnp.broadcast_to(
+                vown[u][:, k : k + 1].astype(jnp.float32), (1, 128))
+
+    tab_copies[0].wait()
+    for copy in moved:
+        copy.wait()
+    for db in [0] + order:
+        for du in subs:
+            block(db, du, lax.rem(me_u + nsub - du, nsub)).wait_recv()
+        place(own.at[db], base + db * rows, nsub)
+    spec = spectrum(x32[...], dft_v)
+    power = sum(g * g for g in groups(spec))
+    sums = [power[c : c + prow] for c in range(0, base, prow)]
+    part_sum = functools.reduce(jnp.add, sums)
+    sums = [power[c : c + rows] for c in range(base, base + nblk * rows, rows)]
+    own_sum = functools.reduce(jnp.add, sums)
+    high, low = split(jnp.concatenate([part_sum, own_sum], axis=0))
+    total = mxu(jnp.concatenate([high, low], axis=0), band_ones())
+    level = (total[: prow + rows] + total[prow + rows :]) * (1.0 / (BAND * nblk))
+    factor = jnp.tile(lax.rsqrt(level + eps) * vcol[...], (1, 8))
+    row_id = lax.broadcasted_iota(jnp.int32, (prow, 1), 0) // wide
+    partner = []
+    for db in range(nblk):
+        w = jnp.zeros((prow, 1), jnp.float32)
+        seg = lax.rem(me_b + nblk - db, nblk)
+        for n in range(nblk):
+            w = jnp.where(row_id == n, select[0, n, seg].astype(jnp.float32), w)
+        partner.append(rounded(spec[db * prow : (db + 1) * prow] * factor[:prow]) * w)
+
+    acc_re = [0.0] * rows
+    acc_im = [0.0] * rows
+    for db in range(nblk):
+        first = base + db * rows
+        a = rounded(spec[first : first + rows] * factor[prow:])
+        br, bi = partner[db][:, :BINS], partner[db][:, BINS:]
+        for i in range(rows):
+            ar, ai = a[i : i + 1, :BINS], a[i : i + 1, BINS:]
+            acc_re[i] = acc_re[i] + (ar * br + ai * bi)
+            acc_im[i] = acc_im[i] + (ai * br - ar * bi)
+    stacked = jnp.concatenate(
+        [jnp.concatenate(acc_re, axis=0), jnp.concatenate(acc_im, axis=0)], axis=1)
+    tab_copies[1].wait()
+    out[...] = lags_of(stacked, lag_v)
+    for copy in sent:
+        copy.wait_send()
+
+
+def fused(nblk, nsub, raw, valid, select):
+    wide = raw.shape[1]
+    rows, prow = wide * nsub, wide * nblk
+    tables = (
+        jnp.asarray(dft_split()),
+        jnp.asarray(lag_split(1.0 / math.sqrt(BINS * nblk))),
+    )
+    hbm = pl.BlockSpec(memory_space=pltpu.HBM)
+    result = pl.pallas_call(
+        functools.partial(kernel, nblk, nsub, wide),
+        out_shape=jax.ShapeDtypeStruct((rows * prow, LAGS), jnp.float32),
+        in_specs=[hbm] * 5,
+        out_specs=pl.BlockSpec(memory_space=pltpu.VMEM),
+        scratch_shapes=[
+            pltpu.SMEM(select.shape, jnp.int32),
+            pltpu.VMEM((nblk, nblk, wide, SEG_LEN), jnp.bfloat16),
+            pltpu.VMEM((nblk, nsub, wide, SEG_LEN), jnp.bfloat16),
+            pltpu.VMEM((nblk, 1, wide), jnp.int32),
+            pltpu.VMEM((nsub, 1, wide), jnp.int32),
+            pltpu.VMEM((nblk * (rows + prow), SEG_LEN), jnp.float32),
+            pltpu.VMEM((rows + prow, 128), jnp.float32),
+            pltpu.VMEM((2, 3 * QUARTER, BINS), jnp.bfloat16),
+            pltpu.VMEM((2, 3 * QUARTER, LAGS), jnp.bfloat16),
+            pltpu.SemaphoreType.DMA((nblk,)),
+            pltpu.SemaphoreType.DMA((nblk,)),
+            pltpu.SemaphoreType.DMA((nblk + nsub,)),
+            pltpu.SemaphoreType.DMA((nblk + nsub,)),
+            pltpu.SemaphoreType.DMA((nblk, nsub)),
+            pltpu.SemaphoreType.DMA((nblk, nsub)),
+            pltpu.SemaphoreType.DMA((5,)),
+            pltpu.SemaphoreType.DMA((2,)),
+        ],
+        compiler_params=pltpu.CompilerParams(
+            collective_id=0, has_side_effects=True, vmem_limit_bytes=32 * 2**20
+        ),
+    )(*(pltpu.with_memory_space_constraint(a, pltpu.HBM) for a in (raw, valid, select) + tables))
+    return result.reshape(rows, nblk, wide, LAGS)
 
 
 def dft_tables(length, bins):
@@ -54,21 +333,27 @@
     return jnp.stack([real, imag], axis=3)
 
 
-def per_device(raw, valid, select):
+def by_collectives(raw, valid, select):
     regrouped = lax.all_to_all(raw, "blk", split_axis=0, concat_axis=2, tiled=True)
     spectra = whiten(regrouped, valid, SEG_LEN, BAND)
     segs = spectra.shape[1]
-    bins = SEG_LEN // 2
-    table = lag_table(bins, LAGS, SEG_LEN, 1.0 / math.sqrt(bins * segs))
-    weight_rows = select[0]
+    table = lag_table(BINS, LAGS, SEG_LEN, 1.0 / math.sqrt(BINS * segs))
     block = lax.all_gather(spectra, "sub", axis=0, tiled=True)
     stacked = pair_terms(
-        block, weight_rows, lax.all_gather(spectra[None], "blk", axis=0, tiled=True)
+        block, select[0], lax.all_gather(spectra[None], "blk", axis=0, tiled=True)
     )
     return jnp.einsum("injrf,rfl->injl", stacked, table, precision=lax.Precision.HIGHEST)
 
 
 def solution(mesh):
+    nblk, nsub = mesh.shape["blk"], mesh.shape["sub"]
+
+    def per_device(raw, valid, select):
+        fits = raw.shape[2] == SEG_LEN and raw.shape[0] == nblk and nblk * nsub <= 16
+        if fits:
+            return fused(nblk, nsub, raw, valid, select)
+        return by_collectives(raw, valid, select)
+
     return jax.shard_map(
         per_device,
         mesh=mesh,

time: 74 us -> 12.7 us (0.17)
  matrix products: 30.9 us -> 0 us
  blocking collectives: 19.1 us -> 0 us
  Pallas kernels: 0 us -> 11.8 us
  other arithmetic: 8.5 us -> 0 us
  local copies, waits for them, and re-layouts: 8.68 us -> 0.73 us
  starting transfers between devices: 6.45 us -> 0 us
    dot_general x4 -> x0, matrix products: 30.9 us -> none  [the longest x1 10.9 us: pair_terms(): jnp.einsum('isaf,njsbf->injabf', own, masked, preferred_element_type=jnp....]
    all_gather x2 -> x0, blocking collectives: 19.1 us -> none  [the longest x1 13.7 us: per_device(): lax.all_gather(spectra[None], 'blk', axis=0, tiled=True)]
    pallas_call x0 -> x1, Pallas kernels: none -> 11.8 us  [fused(): pl.pallas_call(functools.partial(kernel, nblk, nsub, wide), out_shape=jax...]
    all_to_all x1 -> x0, starting transfers between devices: 6.45 us -> none  [per_device(): lax.all_to_all(raw, 'blk', split_axis=0, concat_axis=2, tiled=True)]
    mul x4 -> x0, other arithmetic: 5.18 us -> none  [the longest x1 5.06 us: lag_table(): return jnp.stack([weight * jnp.cos(angle), -weight * jnp.sin(angle)])]
    all_gather x1 -> x0, local copies, waits for them, and re-layouts: 2.93 us -> none  [per_device(): block = lax.all_gather(spectra, 'sub', axis=0, tiled=True)]
    add x1 -> x0, other arithmetic: 2.43 us -> none  [pair_terms(): real = prod[:, :, :, 0, 0] + prod[:, :, :, 1, 1]]
    mul x3 -> x0, local copies, waits for them, and re-layouts: 2.08 us -> none  [the longest x1 1.92 us: pair_terms(): masked = piece * weight_rows.astype(jnp.bfloat16)[:, None, :, None, None]]
  transfers between devices with their start and end apart: 1 -> 0, of which waited for: 0 -> 0; matrix products, arithmetic and copies ran while one was open for 8% -> 0% of each run, Pallas kernels for 0% -> 0%
where the time goes in v4:
time: 12.7 us; the launch traced here: 12.5 us
  Pallas kernels  11.8 us (93%)
  local copies, waits for them, and re-layouts  0.73 us (6%)
    pallas_call x1, Pallas kernels, fused(): pl.pallas_call(functools.partial(kernel, nblk, nsub, wide), out_shape=jax...  11.8 us
    reshape x1, local copies, waits for them, and re-layouts, fused(): return result.reshape(rows, nblk, wide, LAGS)  0.73 us

profile of v4, /device:TPU:0, one launch (start us, length us, event | category | flops | bytes accessed | tf_op | source)
XLA Modules:
  0.0 12.5 jit_solution(10393885358623337946)
XLA Ops:
  0.0 11.8 %shard_map.55 = f32[64,512]{1,0:T(8,128)S(1)} custom-call(bf16[4,2,1024]{2,1,0:T(2,128)(2,1)} %raw.1, s32[1,2]{1,0:T(1,128)} %valid.1, s32[1,4,4]{2,1,0:T(4,128)} %choose.1, bf16[2,768,512]{2,1,0:T(8,128)(2,1)} %constant.4.clone.dft, bf16[2,768,512]{2,1,0:T(8,128)(2,1)} %constant.5.clone.lag), custom_call_target="tpu_custom_call" | custom-call | tf_op jit(solution)/shard_map/pallas_call | solution.py:264
  11.8 0.7 %reshape.3 = f32[8,4,2,512]{3,2,1,0:T(2,128)} reshape(f32[64,512]{1,0:T(8,128)S(1)} %shard_map.55) | data formatting | bytes 262144 | tf_op jit(solution)/shard_map/reshape | solution.py:292

commit v5 on v4

--- a/solution.py
+++ b/solution.py
@@ -153,7 +153,7 @@
 
     def samples(db):
         return pltpu.make_async_remote_copy(
-            raw, part.at[db], send.at[db], recv.at[db],
+            part.at[0], part.at[db], send.at[db], recv.at[db],
             device_id=at_blk(db), device_id_type=MESH)
 
     def valid_blk(db, at_b):
@@ -169,13 +169,16 @@
     def block(db, du, at_u):
         there = at_blk(db)
         return pltpu.make_async_remote_copy(
-            raw.at[there["blk"]], own.at[db, at_u], fsend.at[db, du], frecv.at[db, du],
+            part.at[0, there["blk"]], own.at[db, at_u], fsend.at[db, du], frecv.at[db, du],
             device_id={**there, **at_sub(du)}, device_id_type=MESH)
 
+    for copy in mine:
+        copy.wait()
     sent = [samples(db) for db in order]
     sent += [valid_blk(db, me_b) for db in order]
     sent += [valid_sub(du, me_u) for du in subs]
-    sent += [block(db, du, me_u) for db in range(nblk) for du in subs]
+    sent += [block(db, du, me_u) for db in order for du in subs]
+    sent += [block(0, du, me_u) for du in subs]
     for copy in sent + tab_copies:
         copy.start()
 
@@ -184,8 +187,6 @@
             x32[pl.ds(base + c * wide, wide), :] = ref[c].astype(jnp.float32)
 
     base = nblk * prow
-    for copy in mine:
-        copy.wait()
     place(part.at[0], 0, nblk)
     moved = []
     for db in order:

time: 12.7 us -> 12.5 us (0.984)
  Pallas kernels: 11.8 us -> 11.6 us
    pallas_call x1, Pallas kernels: 11.8 us -> 11.6 us  [fused(): pl.pallas_call(functools.partial(kernel, nblk, nsub, wide), out_shape=jax...]
where the time goes in v5:
time: 12.5 us; the launch traced here: 12.3 us
  Pallas kernels  11.6 us (93%)
  local copies, waits for them, and re-layouts  0.73 us (6%)
    pallas_call x1, Pallas kernels, fused(): pl.pallas_call(functools.partial(kernel, nblk, nsub, wide), out_shape=jax...  11.6 us
    reshape x1, local copies, waits for them, and re-layouts, fused(): return result.reshape(rows, nblk, wide, LAGS)  0.73 us

profile of v5, /device:TPU:0, one launch (start us, length us, event | category | flops | bytes accessed | tf_op | source)
XLA Modules:
  0.0 12.3 jit_solution(3585734941635632829)
XLA Ops:
  0.0 11.6 %shard_map.55 = f32[64,512]{1,0:T(8,128)S(1)} custom-call(bf16[4,2,1024]{2,1,0:T(2,128)(2,1)} %raw.1, s32[1,2]{1,0:T(1,128)} %valid.1, s32[1,4,4]{2,1,0:T(4,128)} %choose.1, bf16[2,768,512]{2,1,0:T(8,128)(2,1)} %constant.4.clone.dft, bf16[2,768,512]{2,1,0:T(8,128)(2,1)} %constant.5.clone.lag), custom_call_target="tpu_custom_call" | custom-call | tf_op jit(solution)/shard_map/pallas_call | solution.py:265
  11.6 0.7 %reshape.3 = f32[8,4,2,512]{3,2,1,0:T(2,128)} reshape(f32[64,512]{1,0:T(8,128)S(1)} %shard_map.55) | data formatting | bytes 262144 | tf_op jit(solution)/shard_map/reshape | solution.py:293

commit v6 on v5

--- a/solution.py
+++ b/solution.py
@@ -211,6 +211,7 @@
                 vown[u][:, k : k + 1].astype(jnp.float32), (1, 128))
 
     tab_copies[0].wait()
+    tab_copies[1].wait()
     for copy in moved:
         copy.wait()
     for db in [0] + order:
@@ -236,20 +237,20 @@
             w = jnp.where(row_id == n, select[0, n, seg].astype(jnp.float32), w)
         partner.append(rounded(spec[db * prow : (db + 1) * prow] * factor[:prow]) * w)
 
-    acc_re = [0.0] * rows
-    acc_im = [0.0] * rows
+    owns = []
     for db in range(nblk):
         first = base + db * rows
-        a = rounded(spec[first : first + rows] * factor[prow:])
-        br, bi = partner[db][:, :BINS], partner[db][:, BINS:]
-        for i in range(rows):
-            ar, ai = a[i : i + 1, :BINS], a[i : i + 1, BINS:]
-            acc_re[i] = acc_re[i] + (ar * br + ai * bi)
-            acc_im[i] = acc_im[i] + (ai * br - ar * bi)
-    stacked = jnp.concatenate(
-        [jnp.concatenate(acc_re, axis=0), jnp.concatenate(acc_im, axis=0)], axis=1)
-    tab_copies[1].wait()
-    out[...] = lags_of(stacked, lag_v)
+        owns.append(rounded(spec[first : first + rows] * factor[prow:]))
+    parts = []
+    for i in range(rows):
+        real, imag = 0.0, 0.0
+        for db in range(nblk):
+            br, bi = partner[db][:, :BINS], partner[db][:, BINS:]
+            ar, ai = owns[db][i : i + 1, :BINS], owns[db][i : i + 1, BINS:]
+            real = real + (ar * br + ai * bi)
+            imag = imag + (ai * br - ar * bi)
+        parts.append(jnp.concatenate([real, imag], axis=1))
+    out[...] = lags_of(jnp.concatenate(parts, axis=0), lag_v)
     for copy in sent:
         copy.wait_send()
 

time: 12.5 us -> 12.4 us (level)
  no operation moved by 1% of the time
where the time goes in v6:
time: 12.4 us; the launch traced here: 12.2 us
  Pallas kernels  11.5 us (93%)
  local copies, waits for them, and re-layouts  0.73 us (6%)
    pallas_call x1, Pallas kernels, fused(): pl.pallas_call(functools.partial(kernel, nblk, nsub, wide), out_shape=jax...  11.5 us
    reshape x1, local copies, waits for them, and re-layouts, fused(): return result.reshape(rows, nblk, wide, LAGS)  0.73 us

profile of v6, /device:TPU:0, one launch (start us, length us, event | category | flops | bytes accessed | tf_op | source)
XLA Modules:
  0.0 12.2 jit_solution(17290197686219915215)
XLA Ops:
  0.0 11.5 %shard_map.55 = f32[64,512]{1,0:T(8,128)S(1)} custom-call(bf16[4,2,1024]{2,1,0:T(2,128)(2,1)} %raw.1, s32[1,2]{1,0:T(1,128)} %valid.1, s32[1,4,4]{2,1,0:T(4,128)} %choose.1, bf16[2,768,512]{2,1,0:T(8,128)(2,1)} %constant.4.clone.dft, bf16[2,768,512]{2,1,0:T(8,128)(2,1)} %constant.5.clone.lag), custom_call_target="tpu_custom_call" | custom-call | tf_op jit(solution)/shard_map/pallas_call | solution.py:266
  11.5 0.7 %reshape.3 = f32[8,4,2,512]{3,2,1,0:T(2,128)} reshape(f32[64,512]{1,0:T(8,128)S(1)} %shard_map.55) | data formatting | bytes 262144 | tf_op jit(solution)/shard_map/reshape | solution.py:294

commit v7 on v6

--- a/solution.py
+++ b/solution.py
@@ -187,16 +187,6 @@
             x32[pl.ds(base + c * wide, wide), :] = ref[c].astype(jnp.float32)
 
     base = nblk * prow
-    place(part.at[0], 0, nblk)
-    moved = []
-    for db in order:
-        samples(db).wait_recv()
-        keep = pltpu.make_async_copy(
-            part.at[db, me_b], own.at[db, me_u], fsend.at[db, 0])
-        keep.start()
-        moved.append(keep)
-        place(part.at[db], db * prow, nblk)
-
     for db in blks:
         valid_blk(db, lax.rem(me_b + nblk - db, nblk)).wait_recv()
     for du in subs:
@@ -209,6 +199,15 @@
         for k in range(wide):
             vcol[pl.ds(prow + u * wide + k, 1), :] = jnp.broadcast_to(
                 vown[u][:, k : k + 1].astype(jnp.float32), (1, 128))
+    place(part.at[0], 0, nblk)
+    moved = []
+    for db in order:
+        samples(db).wait_recv()
+        keep = pltpu.make_async_copy(
+            part.at[db, me_b], own.at[db, me_u], fsend.at[db, 0])
+        keep.start()
+        moved.append(keep)
+        place(part.at[db], db * prow, nblk)
 
     tab_copies[0].wait()
     tab_copies[1].wait()

time: 12.4 us -> 12.4 us (level)
  no operation moved by 1% of the time
where the time goes in v7:
time: 12.4 us; the launch traced here: 12.2 us
  Pallas kernels  11.5 us (93%)
  local copies, waits for them, and re-layouts  0.73 us (6%)
    pallas_call x1, Pallas kernels, fused(): pl.pallas_call(functools.partial(kernel, nblk, nsub, wide), out_shape=jax...  11.5 us
    reshape x1, local copies, waits for them, and re-layouts, fused(): return result.reshape(rows, nblk, wide, LAGS)  0.73 us

profile of v7, /device:TPU:0, one launch (start us, length us, event | category | flops | bytes accessed | tf_op | source)
XLA Modules:
  0.0 12.2 jit_solution(4680714939834947965)
XLA Ops:
  0.0 11.5 %shard_map.55 = f32[64,512]{1,0:T(8,128)S(1)} custom-call(bf16[4,2,1024]{2,1,0:T(2,128)(2,1)} %raw.1, s32[1,2]{1,0:T(1,128)} %valid.1, s32[1,4,4]{2,1,0:T(4,128)} %choose.1, bf16[2,768,512]{2,1,0:T(8,128)(2,1)} %constant.4.clone.dft, bf16[2,768,512]{2,1,0:T(8,128)(2,1)} %constant.5.clone.lag), custom_call_target="tpu_custom_call" | custom-call | tf_op jit(solution)/shard_map/pallas_call | solution.py:265
  11.5 0.7 %reshape.3 = f32[8,4,2,512]{3,2,1,0:T(2,128)} reshape(f32[64,512]{1,0:T(8,128)S(1)} %shard_map.55) | data formatting | bytes 262144 | tf_op jit(solution)/shard_map/reshape | solution.py:293
